TPU v7x, 32 devices: a whole 2x2x4 slice. The times are simulated.
32 devices in a mesh: dp: 2 (over core), expert: 16 (over z, y, x).
Axes of the slice: x: 2, y: 2, z: 4, core: 2. Of those that a mesh axis runs over, the one named last changes fastest.
Arguments:
- queries: bfloat16 [2048, 2048], P('expert', 'dp'), may hold values from -60 to 60
- kv_cache: bfloat16 [256, 4, 128, 256], P('expert', 'dp'), may hold values from -4 to 4
- page_table: int32 [64, 4], P('expert'), may hold values from 0 to 15, as said below
- lengths: int32 [64], P('expert'), may hold values from 2 to 512, as said below
- residual: bfloat16 [2048, 2048], P('expert', 'dp'), may hold values from -0.59765625 to 0.59765625
- out_proj: bfloat16 [2048, 2048], P('dp'), may hold values from -0.125 to 0.125
- norm_gain: float32 [2048], replicated, may hold values from 0.5 to 1.5
- router: bfloat16 [2048, 64], replicated, may hold values from -0.09375 to 0.09375
- routes: int32 [2048, 6], P('expert'), may hold values from 0 to 63, all different within a row; in each aligned block of 64 rows (0 to 63, 64 to 127, ...) at most 12 rows name the same one
- placement: int32 [64, 2], replicated, may hold values from 0 to 127, as said below
- parity: int32 [64], replicated, may hold values 0 or 1
- slot_in: bfloat16 [2, 128, 2048, 2, 704], P('dp', 'expert'), may hold values from -0.125 to 0.125
- slot_out: bfloat16 [2, 128, 704, 2048], P('dp', 'expert'), may hold values from -0.625 to 0.625
- shared_in: bfloat16 [2048, 2, 1408], P(None, None, 'dp'), may hold values from -0.125 to 0.125
- shared_out: bfloat16 [1408, 2048], P('dp'), may hold values from -0.15625 to 0.15625
Outputs:
- layer_out: bfloat16 [2048, 2048], P('expert', 'dp')
Inputs may be any that keep to these rules, and one draw needn't show every extreme that they name: `page_table`: rows 4 j to 4 j + 3 together hold every number of 0 to 15 once. `lengths`: entry 4 j is at least 125; each aligned group of 4 entries holds one equal to 512. `routes`: the 6 entries of a row differ; in each aligned block of 64 rows no expert is named by more than 12 rows. `placement`: its 128 entries hold every slot once.
All inputs are finite; a program needn't handle non-finite values.
Results may differ from a plain program's by a relative error of at most 0.012.
Values may be sent and summed in bfloat16 or wider, within the bound.
A program may use at most 256 MiB of HBM per device.

v0:
```python
import jax
import jax.numpy as jnp
from jax import lax
from jax.sharding import PartitionSpec as P

D = 2048
HEADS = 16
KV_HEADS = 4
HEAD_DIM = 128
EXPERTS = 64
PAGE = 128
PRE = 125
BLOCK = 64
MOST = 12
masked_score = -1e30
epsilon = 1e-06


def key_owners(table, pool_pages):
    request_count = table.shape[0]
    page_width = table.shape[1]
    page_ids = jnp.arange(pool_pages, dtype=jnp.int32)
    matches = (table[None, :, :] == page_ids[:, None, None]).astype(jnp.int32)
    owners = jnp.sum(
        matches * jnp.arange(request_count, dtype=jnp.int32)[None, :, None], axis=(1, 2)
    )
    ordinal = jnp.sum(matches * jnp.arange(page_width, dtype=jnp.int32)[None, None, :], axis=(1, 2))
    offsets = jnp.arange(PAGE, dtype=jnp.int32)
    key_request = jnp.repeat(owners, PAGE)
    key_position = (ordinal[:, None] * PAGE + offsets[None, :]).reshape(-1)
    return (key_request, key_position)


def row_places(lengths, row_count):
    local = jnp.arange(row_count, dtype=jnp.int32)
    request = jnp.where(local < PRE, 0, local - PRE + 1)
    request_ids = jnp.arange(lengths.shape[0], dtype=jnp.int32)
    picked = jnp.sum(
        jnp.where(request[:, None] == request_ids[None, :], lengths[None, :], 0), axis=1
    )
    position = jnp.where(local < PRE, lengths[0] - PRE + local, picked - 1)
    return (request, position)


def attend(queries, cache, visible):
    row_count = queries.shape[0]
    pages, local_kv, page_len, _ = cache.shape
    sharing = HEADS // KV_HEADS
    keys = cache[..., :HEAD_DIM]
    values = cache[..., HEAD_DIM:]
    query_heads = queries.reshape(row_count, local_kv, sharing, HEAD_DIM)
    scores = jnp.einsum("rkgd,pkod->rkgpo", query_heads, keys, preferred_element_type=jnp.float32)
    scores = scores.reshape(row_count, local_kv, sharing, pages * page_len) * HEAD_DIM ** (-0.5)
    allowed = visible[:, None, None, :]
    scores = jnp.where(allowed, scores, masked_score)
    highest = jnp.max(scores, axis=-1)
    weights = jnp.where(allowed, jnp.exp(scores - highest[..., None]), 0.0)
    weight_sum = jnp.sum(weights, axis=-1)
    rounded = weights.astype(jnp.bfloat16).reshape(row_count, local_kv, sharing, pages, page_len)
    weighted = jnp.einsum("rkgpo,pkod->rkgd", rounded, values, preferred_element_type=jnp.float32)
    attention = (weighted / weight_sum[..., None]).astype(jnp.bfloat16)
    return attention.reshape(row_count, local_kv * sharing * HEAD_DIM)


def route_slots(routes, placement, parity, local):
    picked = (routes[:, :, None] == jnp.arange(EXPERTS, dtype=jnp.int32)[None, None, :]).astype(
        jnp.int32
    )
    flipped = jnp.sum(picked * parity[None, None, :], axis=-1)
    replica = (local[:, None] // BLOCK + flipped) % 2
    first_slot = jnp.sum(picked * placement[None, None, :, 0], axis=-1)
    second_slot = jnp.sum(picked * placement[None, None, :, 1], axis=-1)
    slot_ids = jnp.where(replica == 0, first_slot, second_slot)
    counts = jnp.sum(picked, axis=1).reshape(-1, BLOCK, EXPERTS)
    earlier = jnp.tril(jnp.ones((BLOCK, BLOCK), jnp.bfloat16), -1)
    before = (
        jnp.einsum(
            "ts,bse->bte", earlier, counts.astype(jnp.bfloat16), preferred_element_type=jnp.float32
        )
        .astype(jnp.int32)
        .reshape(-1, EXPERTS)
    )
    ranks = jnp.sum(picked * before[:, None, :], axis=-1)
    return (slot_ids, ranks)


def body(
    queries,
    kv_cache,
    page_table,
    lengths,
    residual,
    out_proj,
    norm_gain,
    router,
    routes,
    placement,
    parity,
    slot_in,
    slot_out,
    shared_in,
    shared_out,
):
    dp_count = lax.axis_size("dp")
    dp_place = lax.axis_index("dp")
    column_count = lax.axis_size("expert")
    row_count = queries.shape[0]
    pool_pages = kv_cache.shape[0]
    key_request, key_position = key_owners(page_table, pool_pages)
    request, position = row_places(lengths, row_count)
    visible = (key_request[None, :] == request[:, None]) & (
        key_position[None, :] <= position[:, None]
    )
    own_heads = attend(queries, kv_cache, visible)
    feature_width = D // dp_count
    projected = jnp.dot(own_heads, out_proj, preferred_element_type=jnp.float32)
    residual_full = lax.dynamic_update_slice(
        jnp.zeros_like(projected),
        residual.astype(jnp.float32),
        (jnp.zeros((), jnp.int32), dp_place * feature_width),
    )
    hidden_state = lax.psum(projected + residual_full, "dp").astype(jnp.bfloat16)
    state_float = hidden_state.astype(jnp.float32)
    mean_square = jnp.mean(state_float * state_float, axis=-1, keepdims=True)
    normed = (state_float * norm_gain[None, :] * lax.rsqrt(mean_square + epsilon)).astype(
        jnp.bfloat16
    )
    logits = jnp.dot(normed, router, preferred_element_type=jnp.float32)
    picked = routes[:, :, None] == jnp.arange(EXPERTS, dtype=jnp.int32)[None, None, :]
    chosen = jnp.sum(jnp.where(picked, logits[:, None, :], 0.0), axis=-1)
    sigmoids = jax.nn.sigmoid(chosen)
    gates = sigmoids / jnp.sum(sigmoids, axis=-1, keepdims=True)
    slots_here = slot_in.shape[1]
    half_units = slot_in.shape[4]
    slot_group = slots_here * column_count
    row_ids = jnp.arange(row_count, dtype=jnp.int32)
    slot_ids, ranks = route_slots(routes, placement, parity, row_ids)
    buffer_rows = slot_group * MOST
    targets = jnp.where(
        slot_ids // slot_group == dp_place // 2, slot_ids % slot_group * MOST + ranks, buffer_rows
    )
    source = (
        jnp.full((buffer_rows + 1,), row_count, jnp.int32)
        .at[targets.reshape(-1)]
        .set(jnp.broadcast_to(row_ids[:, None], targets.shape).reshape(-1))
    )
    gate_table = (
        jnp.zeros((buffer_rows + 1,), jnp.float32).at[targets.reshape(-1)].set(gates.reshape(-1))
    )
    source = source[:buffer_rows]
    gate_table = gate_table[:buffer_rows]
    padded = jnp.concatenate([normed, jnp.zeros((1, D), jnp.bfloat16)], axis=0)
    outgoing = padded[source].reshape(column_count, slots_here, MOST, D)
    weights_in = slot_in[0].reshape(slots_here, D, 2 * half_units)
    gate_up = jnp.einsum(
        "cumd,udh->cumh",
        lax.all_to_all(outgoing, "expert", split_axis=0, concat_axis=0, tiled=True),
        weights_in,
        preferred_element_type=jnp.float32,
    )
    hidden_units = (jax.nn.silu(gate_up[..., :half_units]) * gate_up[..., half_units:]).astype(
        jnp.bfloat16
    )
    returned = lax.all_to_all(
        jnp.einsum(
            "cumh,uhd->cumd", hidden_units, slot_out[0], preferred_element_type=jnp.float32
        ).astype(jnp.bfloat16),
        "expert",
        split_axis=0,
        concat_axis=0,
        tiled=True,
    )
    weighted_rows = returned.reshape(buffer_rows, D).astype(jnp.float32) * gate_table[:, None]
    routed = jax.ops.segment_sum(weighted_rows, source, num_segments=row_count + 1)[:row_count]
    shared_width = shared_in.shape[2]
    shared_gate_up = jnp.dot(
        normed, shared_in.reshape(D, 2 * shared_width), preferred_element_type=jnp.float32
    )
    shared_hidden = (
        jax.nn.silu(shared_gate_up[:, :shared_width]) * shared_gate_up[:, shared_width:]
    ).astype(jnp.bfloat16)
    shared_part = jnp.dot(shared_hidden, shared_out, preferred_element_type=jnp.float32)
    summed = lax.psum_scatter(
        (routed + shared_part).astype(jnp.bfloat16), "dp", scatter_dimension=1, tiled=True
    ).astype(jnp.float32)
    own_state = lax.dynamic_slice_in_dim(state_float, dp_place * feature_width, feature_width, 1)
    return (own_state + summed).astype(jnp.bfloat16)


def solution(mesh):
    in_specs = (
        P("expert", "dp"),
        P("expert", "dp", None, None),
        P("expert", None),
        P("expert"),
        P("expert", "dp"),
        P("dp", None),
        P(),
        P(),
        P("expert", None),
        P(),
        P(),
        P("dp", "expert", None, None, None),
        P("dp", "expert", None, None),
        P(None, None, "dp"),
        P("dp", None),
    )
    out_specs = P("expert", "dp")
    return jax.shard_map(body, mesh=mesh, in_specs=in_specs, out_specs=out_specs, check_vma=False)
```

profile of v0, /device:TPU:0, one launch (start us, length us, event | category | flops | bytes accessed | tf_op | source)
XLA Modules:
  0.0 483.3 jit_solution(14522558699175085918)
XLA Ops:
  6.5 0.0 copy-start
  6.5 0.9 convert_reduce_fusion
  7.4 0.1 convert_element_type.69
  7.5 0.2 fusion.25
  7.7 0.1 copy.70
  7.8 0.1 mul.152
  7.9 0.8 slice_bitcast_fusion.1
  8.6 0.8 select_reduce_fusion.4
  9.5 0.1 copy.71
  9.6 0.1 reduce_sum.125
  9.7 0.1 copy.67
  9.9 0.1 reduce_sum.120
  10.0 0.1 copy.68
  10.1 0.1 reduce_sum.122
  10.3 0.1 copy.66
  10.4 0.1 add.205
  10.6 0.1 reshape.377
  10.7 0.1 fusion.54
  10.8 3.4 scatter_custom_fusion
  14.2 0.8 select_reduce_fusion.6
  15.0 0.1 iota_add_fusion
  15.0 1.1 reshape.356
  16.1 3.1 fusion.65
  19.3 2.3 copy.90
  21.6 0.7 select_reduce_fusion.7
  23.0 0.5 compare_and_fusion
  23.5 2.7 fusion.4
  26.1 2.0 fusion.8
  28.2 0.0 copy-start.5
  28.2 0.0 copy-start.7
  28.2 2.2 fusion.33
  30.4 0.0 copy-start.9
  30.4 1.7 fusion.66
  32.2 1.9 add_dynamic-update-slice_fusion
  34.1 7.5 %all-reduce.2 = bf16[128,2048]{1,0:T(8,128)(2,1)S(1)} all-reduce(f32[128,2048]{1,0:T(8,128)} %add_dynamic-update-slice_fusion), channel_id=1, replica_groups=mesh['dp'=2,'expert'=16] {'dp'}, use_global_device_ids=true, to_apply=%region_5.6 | all-reduce | flops 262144 | bytes 1572864 | tf_op jit(solution)/shard_map/psum | solution.py:122
  41.6 0.2 multiply_reduce_fusion
  41.8 0.6 copy-done.1
  42.4 0.0 copy-done.9
  42.4 0.2 multiply_convert_fusion
  42.6 0.8 copy-done.3
  43.4 7.1 %gather_fusion = bf16[1536,2048]{1,0:T(8,128)(2,1)} fusion(bf16[129,2048]{1,0:T(8,128)(2,1)S(1)} %concatenate.3, s32[2048]{0:T(1024)S(1)} %pad_clamp_fusion), kind=kCustom, calls=%fused_computation | custom fusion | bytes 12589056 | tf_op jit(solution)/shard_map/gather | solution.py:153
  50.5 10.6 %reshape.359 = bf16[16,8,12,2048]{3,2,1,0:T(8,128)(2,1)} reshape(bf16[1536,2048]{1,0:T(8,128)(2,1)} %gather_fusion) | data formatting | bytes 12582912 | tf_op jit(solution)/shard_map/reshape | solution.py:153
  61.1 7.5 %copy.72 = bf16[16,8,12,2048]{3,1,2,0:T(8,128)(2,1)S(1)} copy(bf16[16,8,12,2048]{3,2,1,0:T(8,128)(2,1)} %reshape.359) | data formatting | bytes 12582912 | tf_op jit(solution)/shard_map/reshape | solution.py:153
  68.6 147.5 %all_to_all.10 = bf16[16,8,12,2048]{3,1,2,0:T(8,128)(2,1)} all-to-all(bf16[16,8,12,2048]{3,1,2,0:T(8,128)(2,1)S(1)} %copy.72), channel_id=1, replica_groups=mesh['dp'=2,'expert'=16] {'expert'}, dimensions={0} | all-to-all | bytes 12582912 | tf_op jit(solution)/shard_map/all_to_all | solution.py:157
  216.1 27.7 %fusion.10 = f32[16,8,12,1408]{3,0,2,1:T(8,128)} fusion(bf16[8,2048,1408,1]{1,2,3,0:T(8,128)(2,1)} %bitcast.94, bf16[16,8,12,2048]{3,1,2,0:T(8,128)(2,1)} %all_to_all.10), kind=kOutput, calls=%fused_computation.17 | convolution fusion | flops 8858370048 | bytes 61079552 | tf_op jit(solution)/shard_map/cumd,udh->cumh/dot_general | solution.py:155
  243.8 15.2 %convert_bitcast_fusion = bf16[16,8,12,2048]{3,0,2,1:T(8,128)(2,1)} fusion(bf16[1,8,704,2048]{3,2,1,0:T(8,128)(2,1)} %param.27, f32[16,8,12,1408]{3,0,2,1:T(8,128)} %fusion.10), kind=kOutput, calls=%fused_computation.14 | convolution fusion | flops 4438818816 | bytes 38797312 | tf_op jit(solution)/shard_map/cumh,uhd->cumd/dot_general | solution.py:165
  259.0 8.9 %copy.75 = bf16[16,8,12,2048]{3,1,2,0:T(8,128)(2,1)} copy(bf16[16,8,12,2048]{3,0,2,1:T(8,128)(2,1)} %convert_bitcast_fusion) | data formatting | bytes 12582912 | tf_op jit(solution)/shard_map/convert_element_type | solution.py:167
  267.9 4.8 all-to-all-start.1
  272.6 0.2 reduce-scatter.2.cloned.1.call-start
  272.9 1.3 fusion.67
  274.1 0.0 copy-done.8
  274.2 0.1 copy.77
  274.3 0.1 reshape.385
  274.5 3.4 scatter_custom_fusion.1
  277.9 5.5 %fusion.68 = f32[128,1408]{1,0:T(8,128)} fusion(bf16[128,2048]{1,0:T(8,128)(2,1)S(1)} %copy-done.4, bf16[2048,1408]{0,1:T(8,128)(2,1)} %bitcast.90), kind=kOutput, calls=%fused_computation.111 | convolution fusion | flops 738197504 | bytes 7012352 | tf_op jit(solution)/shard_map/dot_general | solution.py:176
  283.4 104.6 %all-to-all-done.1 = bf16[16,8,12,2048]{3,1,2,0:T(8,128)(2,1)} async-done(((bf16[16,8,12,2048]{3,1,2,0:T(8,128)(2,1)}), bf16[16,8,12,2048]{3,1,2,0:T(8,128)(2,1)}, u32[]{:S(2)}, u32[]{:S(2)}) %all-to-all-start.1) | async-done | bytes 6291488 | tf_op jit(solution)/shard_map/all_to_all | solution.py:164
  387.9 13.7 %copy.76 = f32[16,8,12,2048]{3,2,1,0:T(8,128)} copy(bf16[16,8,12,2048]{3,1,2,0:T(8,128)(2,1)} %all-to-all-done.1) | data formatting | bytes 18874368 | tf_op jit(solution)/shard_map/convert_element_type | solution.py:173
  401.6 15.7 %reshape.362 = f32[1536,2048]{1,0:T(8,128)} reshape(f32[16,8,12,2048]{3,2,1,0:T(8,128)} %copy.76) | data formatting | bytes 25165824 | tf_op jit(solution)/shard_map/convert_element_type | solution.py:173
  417.4 23.1 %scatter_custom_fusion.2 = f32[129,2048]{1,0:T(8,128)} fusion(s32[1536]{0:T(1024)S(1)} %get-tuple-element.14, f32[1536,2048]{1,0:T(8,128)} %reshape.362, f32[1536]{0:T(1024)S(1)} %bitcast.93, f32[]{:T(128)} %constant.114.clone.1), kind=kCustom, calls=%fused_computation.6 | custom fusion | flops 6291456 | bytes 13647876 | tf_op jit(solution)/shard_map/scatter-add | solution.py:174
  440.5 2.9 fusion.19
  443.4 0.0 reduce-scatter.2.cloned.1.call-update
  443.4 1.1 convert_element_type.112
  444.5 29.9 %reduce-scatter.2.cloned.1.call-done = bf16[128,1024]{1,0:T(8,128)(2,1)} async-done(((bf16[128,2048]{1,0:T(8,128)(2,1)}), bf16[128,1024]{1,0:T(8,128)(2,1)}) %reduce-scatter.2.cloned.1.call-update) | async-done | bytes 262160 | tf_op jit(solution)/shard_map/reduce_scatter | solution.py:183
  474.4 1.9 add_convert_fusion
  (26 shorter events, 0.2 us)
Async XLA Ops:
  6.5 434.0 %copy-start = (bf16[704,2048]{1,0:T(8,128)(2,1)S(1)}, bf16[704,2048]{1,0:T(8,128)(2,1)}, u32[]{:S(2)}) copy-start(bf16[704,2048]{1,0:T(8,128)(2,1)} %param.29) | copy-start | bytes 8650756
  23.5 4.7 copy-start.6
  28.2 2.2 copy-start.5
  28.2 4.0 copy-start.7
  30.4 12.0 %copy-start.9 = (f32[2048]{0:T(1024)S(1)}, f32[2048]{0:T(1024)}, u32[]{:S(2)}) copy-start(f32[2048]{0:T(1024)} %param.21) | copy-start | bytes 24580
  41.6 0.8 copy-start.1
  42.6 0.8 copy-start.3
  267.8 5.0 %copy-start.4 = (bf16[128,2048]{1,0:T(8,128)(2,1)S(1)}, bf16[128,2048]{1,0:T(8,128)(2,1)}, u32[]{:S(2)}) copy-start(bf16[128,2048]{1,0:T(8,128)(2,1)} %copy-done.3) | copy-start | bytes 1572868
  267.9 6.3 %copy-start.8 = (s32[128,6]{0,1:T(8,128)S(1)}, s32[128,6]{0,1:T(8,128)}, u32[]{:S(2)}) copy-start(s32[128,6]{0,1:T(8,128)} %param.23) | copy-start | bytes 9220
  267.9 120.1 %all-to-all-start.1 = ((bf16[16,8,12,2048]{3,1,2,0:T(8,128)(2,1)}), bf16[16,8,12,2048]{3,1,2,0:T(8,128)(2,1)}, u32[]{:S(2)}, u32[]{:S(2)}) async-start(bf16[16,8,12,2048]{3,1,2,0:T(8,128)(2,1)} %copy.75), calls=%async_computation.1 | async-start | bytes 12582912 | tf_op jit(solution)/shard_map/all_to_all | solution.py:164
  272.6 201.8 %reduce-scatter.2.cloned.1.call-start = ((), (), s32[]{:S(2)}) async-start(), calls=%async_computation.3 | async-start | bytes 786432 | tf_op jit(solution)/shard_map/reduce_scatter | solution.py:183
  417.4 26.1 %copy-start.2 = (bf16[128,2048]{1,0:T(8,128)(2,1)S(1)}, bf16[128,2048]{1,0:T(8,128)(2,1)}, u32[]{:S(2)}) copy-start(bf16[128,2048]{1,0:T(8,128)(2,1)} %copy-done.1) | copy-start | bytes 1572868
Sparse Core Ops, SparseCore 0:
  443.6 30.7 reduce-scatter.1
where the time goes:
time: 491 us; the launch traced here: 483 us
  blocking collectives  155 us (32%)
  waiting for transfers between devices  134 us (27%)
  local copies, waits for them, and re-layouts  80.7 us (16%)
  matrix products  59.3 us (12%)
  other arithmetic  34.3 us (7%)
  between operations  14.6 us (3%)
  starting transfers between devices  4.97 us (1%)
    all_to_all x1, blocking collectives, body(): lax.all_to_all(outgoing, 'expert', split_axis=0, concat_axis=0, tiled=True)  148 us
    all_to_all x1, waiting for transfers between devices, body(): lax.all_to_all(jnp.einsum('cumh,uhd->cumd', hidden_units, slot_out[0], pr...  105 us
    reduce_scatter x1, waiting for transfers between devices, body(): lax.psum_scatter((routed + shared_part).astype(jnp.bfloat16), 'dp', scatt...  29.9 us
    convert_element_type x2, local copies, waits for them, and re-layouts, body(): returned.reshape(buffer_rows, D).astype(jnp.float32) * gate_table[:, None]  29.5 us
    dot_general x1, matrix products, body(): jnp.einsum('cumd,udh->cumh', lax.all_to_all(outgoing, 'expert', split_axi...  27.7 us
    scatter-add x1, other arithmetic, body(): jax.ops.segment_sum(weighted_rows, source, num_segments=row_count + 1)  23.1 us
    reshape x2, local copies, waits for them, and re-layouts, body(): outgoing = padded[source].reshape(column_count, slots_here, MOST, D)  18.1 us
    dot_general x1, matrix products, body(): jnp.einsum('cumh,uhd->cumd', hidden_units, slot_out[0], preferred_element...  15.2 us
  transfers between devices with their start and end apart: 2, of which 2 were waited for; matrix products, arithmetic and copies ran while one was open for 2% of the time, Pallas kernels for 0%

commit v1 on v0

--- a/solution.py
+++ b/solution.py
@@ -14,6 +14,28 @@
 MOST = 12
 masked_score = -1e30
 epsilon = 1e-06
+
+
+def split_up(x, dim, devices):
+    before, after = (x.shape[:dim], x.shape[dim + 1 :])
+    return jnp.moveaxis(x.reshape(*before, devices, -1, *after), dim, 0)
+
+
+def joined_along(blocks, dim):
+    lengths = list(blocks.shape[1:])
+    lengths[dim] *= blocks.shape[0]
+    return jnp.moveaxis(blocks, 0, dim).reshape(lengths)
+
+
+def sent_to_each(shard, axis, split_dim, concat_dim):
+    length, index = (lax.axis_size(axis), lax.axis_index(axis))
+    parts = split_up(shard, split_dim, length)
+    outs = [parts[index]]
+    for step in range(1, length):
+        sent = parts[(index + step) % length]
+        outs.append(lax.ppermute(sent, axis, [(i, (i + step) % length) for i in range(length)]))
+    parts = jnp.stack(outs)[(index - jnp.arange(length)) % length]
+    return joined_along(parts, concat_dim)
 
 
 def key_owners(table, pool_pages):
@@ -161,14 +183,13 @@
     hidden_units = (jax.nn.silu(gate_up[..., :half_units]) * gate_up[..., half_units:]).astype(
         jnp.bfloat16
     )
-    returned = lax.all_to_all(
+    returned = sent_to_each(
         jnp.einsum(
             "cumh,uhd->cumd", hidden_units, slot_out[0], preferred_element_type=jnp.float32
         ).astype(jnp.bfloat16),
         "expert",
-        split_axis=0,
-        concat_axis=0,
-        tiled=True,
+        0,
+        0,
     )
     weighted_rows = returned.reshape(buffer_rows, D).astype(jnp.float32) * gate_table[:, None]
     routed = jax.ops.segment_sum(weighted_rows, source, num_segments=row_count + 1)[:row_count]

time: 491 us -> 549 us (1.12)
  blocking collectives: 155 us -> 7.35 us
  starting transfers between devices: 4.97 us -> 118 us
  local copies, waits for them, and re-layouts: 80.7 us -> 134 us
  waiting for transfers between devices: 134 us -> 174 us
    all_to_all x1 -> x0, blocking collectives: 148 us -> none  [body(): lax.all_to_all(outgoing, 'expert', split_axis=0, concat_axis=0, tiled=True)]
    ppermute x0 -> x15, starting transfers between devices: none -> 110 us  [sent_to_each(): lax.ppermute(sent, axis, [(i, (i + step) % length) for i in range(length)])]
    ppermute x0 -> x15, waiting for transfers between devices: none -> 52.9 us  [sent_to_each(): lax.ppermute(sent, axis, [(i, (i + step) % length) for i in range(length)])]
    another operation x0 -> x17, local copies, waits for them, and re-layouts: none -> 40.4 us
    reduce_scatter x1, waiting for transfers between devices: 29.9 us -> 12.4 us  [body(): lax.psum_scatter((routed + shared_part).astype(jnp.bfloat16), 'dp', scatt...]
    unnamed x21 -> x38, local copies, waits for them, and re-layouts: 3.71 us -> 15.8 us
    convert_element_type x1 -> x0, local copies, waits for them, and re-layouts: 8.89 us -> none  [body(): returned = lax.all_to_all(jnp.einsum('cumh,uhd->cumd', hidden_units, slot...]
    gather x0 -> x1, local copies, waits for them, and re-layouts: none -> 6.39 us  [sent_to_each(): parts = jnp.stack(outs)[(index - jnp.arange(length)) % length]]
  transfers between devices with their start and end apart: 2 -> 17, of which waited for: 2 -> 6; matrix products, arithmetic and copies ran while one was open for 2% -> 6% of each run, Pallas kernels for 0% -> 0%
where the time goes in v1:
time: 549 us; the launch traced here: 541 us
  waiting for transfers between devices  174 us (32%)
  local copies, waits for them, and re-layouts  134 us (24%)
  starting transfers between devices  118 us (21%)
  matrix products  59.2 us (11%)
  other arithmetic  33.7 us (6%)
  between operations  14.3 us (3%)
  blocking collectives  7.35 us (1%)
    ppermute x15, starting transfers between devices, sent_to_each(): lax.ppermute(sent, axis, [(i, (i + step) % length) for i in range(length)])  110 us
    all_to_all x1, waiting for transfers between devices, body(): lax.all_to_all(outgoing, 'expert', split_axis=0, concat_axis=0, tiled=True)  109 us
    ppermute x15, waiting for transfers between devices, sent_to_each(): lax.ppermute(sent, axis, [(i, (i + step) % length) for i in range(length)])  52.9 us
    another operation x16, local copies, waits for them, and re-layouts  39.7 us
    convert_element_type x2, local copies, waits for them, and re-layouts, body(): returned.reshape(buffer_rows, D).astype(jnp.float32) * gate_table[:, None]  29.3 us
    dot_general x1, matrix products, body(): jnp.einsum('cumd,udh->cumh', lax.all_to_all(outgoing, 'expert', split_axi...  27.6 us
    scatter-add x1, other arithmetic, body(): jax.ops.segment_sum(weighted_rows, source, num_segments=row_count + 1)  23.1 us
    reshape x2, local copies, waits for them, and re-layouts, body(): outgoing = padded[source].reshape(column_count, slots_here, MOST, D)  21.3 us
  transfers between devices with their start and end apart: 17, of which 6 were waited for; matrix products, arithmetic and copies ran while one was open for 6% of the time, Pallas kernels for 0%

profile of v1, /device:TPU:0, one launch (start us, length us, event | category | flops | bytes accessed | tf_op | source)
XLA Modules:
  0.0 541.2 jit_solution(14656461387949841432)
XLA Ops:
  6.6 0.9 convert_reduce_fusion
  8.7 0.8 select_reduce_fusion.4
  10.8 3.4 scatter_custom_fusion
  14.2 0.8 select_reduce_fusion.6
  15.0 1.1 reshape.453
  16.2 3.1 fusion.68
  19.3 2.3 copy.151
  22.2 2.6 fusion.4
  24.8 2.0 fusion.8
  26.9 2.2 fusion.34
  29.1 1.7 fusion.69
  30.8 1.9 add_dynamic-update-slice_fusion
  32.8 7.4 %all-reduce.2 = bf16[128,2048]{1,0:T(8,128)(2,1)S(1)} all-reduce(f32[128,2048]{1,0:T(8,128)} %add_dynamic-update-slice_fusion), channel_id=1, replica_groups=mesh['dp'=2,'expert'=16] {'dp'}, use_global_device_ids=true, to_apply=%region_5.6 | all-reduce | flops 262144 | bytes 1572864 | tf_op jit(solution)/shard_map/psum | solution.py:144
  41.1 0.8 copy-done.3
  42.0 7.1 %gather_fusion = bf16[1536,2048]{1,0:T(8,128)(2,1)} fusion(bf16[129,2048]{1,0:T(8,128)(2,1)S(1)} %concatenate.3, s32[2048]{0:T(1024)S(1)} %pad_clamp_fusion), kind=kCustom, calls=%fused_computation | custom fusion | bytes 12589056 | tf_op jit(solution)/shard_map/gather | solution.py:175
  49.0 10.6 %reshape.456 = bf16[16,8,12,2048]{3,2,1,0:T(8,128)(2,1)} reshape(bf16[1536,2048]{1,0:T(8,128)(2,1)} %gather_fusion) | data formatting | bytes 12582912 | tf_op jit(solution)/shard_map/reshape | solution.py:175
  59.6 10.7 %copy.118 = bf16[16,8,12,2048]{3,1,2,0:T(8,128)(2,1)} copy(bf16[16,8,12,2048]{3,2,1,0:T(8,128)(2,1)} %reshape.456) | data formatting | bytes 12582912 | tf_op jit(solution)/shard_map/reshape | solution.py:175
  70.3 8.2 %all-to-all-start = ((bf16[16,8,12,2048]{3,1,2,0:T(8,128)(2,1)}), bf16[16,8,12,2048]{3,1,2,0:T(8,128)(2,1)}, u32[]{:S(2)}, u32[]{:S(2)}) async-start(bf16[16,8,12,2048]{3,1,2,0:T(8,128)(2,1)} %copy.118), calls=%async_computation | async-start | bytes 12582912 | tf_op jit(solution)/shard_map/all_to_all | solution.py:179
  78.8 1.2 fusion.70
  80.5 3.6 scatter_custom_fusion.1
  84.1 5.5 %fusion.71 = f32[128,1408]{1,0:T(8,128)} fusion(bf16[128,2048]{1,0:T(8,128)(2,1)S(1)} %copy-done.4, bf16[2048,1408]{0,1:T(8,128)(2,1)} %bitcast.168), kind=kOutput, calls=%fused_computation.166 | convolution fusion | flops 738197504 | bytes 7012352 | tf_op jit(solution)/shard_map/dot_general | solution.py:197
  89.6 109.1 %all-to-all-done = bf16[16,8,12,2048]{3,1,2,0:T(8,128)(2,1)} async-done(((bf16[16,8,12,2048]{3,1,2,0:T(8,128)(2,1)}), bf16[16,8,12,2048]{3,1,2,0:T(8,128)(2,1)}, u32[]{:S(2)}, u32[]{:S(2)}) %all-to-all-start) | async-done | bytes 6291488 | tf_op jit(solution)/shard_map/all_to_all | solution.py:179
  198.7 27.6 %fusion.10 = f32[16,8,12,1408]{3,0,2,1:T(8,128)} fusion(bf16[8,2048,1408,1]{1,2,3,0:T(8,128)(2,1)} %bitcast.187, bf16[16,8,12,2048]{3,1,2,0:T(8,128)(2,1)} %all-to-all-done), kind=kOutput, calls=%fused_computation.17 | convolution fusion | flops 8858370048 | bytes 61079552 | tf_op jit(solution)/shard_map/cumd,udh->cumh/dot_general | solution.py:177
  226.4 15.2 %fusion.14 = bf16[8,16,12,2048]{3,1,2,0:T(8,128)(2,1)} fusion(bf16[1,8,704,2048]{3,2,1,0:T(8,128)(2,1)} %param.27, f32[16,8,12,1408]{3,0,2,1:T(8,128)} %fusion.10), kind=kOutput, calls=%fused_computation.20 | convolution fusion | flops 4438818816 | bytes 38797312 | tf_op jit(solution)/shard_map/cumh,uhd->cumd/dot_general | solution.py:187
  241.5 28.7 %constant_dynamic-slice_fusion = (bf16[8,1,12,2048]{3,1,2,0:T(2,128)(2,1)S(1)}, bf16[8,1,12,2048]{3,1,2,0:T(2,128)(2,1)S(1)}, bf16[8,1,12,2048]{3,1,2,0:T(2,128)...) fusion(bf16[8,16,12,2048]{3,1,2,0:T(8,128)(2,1)} %fusion.14, ...), kind=kLoop, calls=%fused_computation.106 | loop fusion | bytes 12582976 | tf_op jit(solution)/shard_map/dynamic-slice.32
  270.2 1.6 copy.197
  271.8 2.4 collective-permute-start
  274.2 1.6 copy.196
  275.7 8.9 %collective-permute-start.1 = (bf16[1,8,12,2048]{3,1,2,0:T(8,128)(2,1)S(1)}, bf16[1,8,12,2048]{3,1,2,0:T(8,128)(2,1)S(1)}, u32[]{:S(2)}, u32[]{:S(2)}) collective-permute-start(bf16[1,8,12,2048]{3,1,2,0:T(8,128)(2,1)S(1)} %bitcast.182), channel_id=1, source_target_pairs={{0,2},{1,3},{2,4},{3,5},{4,6},{5,7},{6,8},{7,9},{8,10},{9,11},{10,... | collective-permute-start | bytes 1179656 | tf_op jit(solution)/shard_map/ppermute | solution.py:36
  284.7 1.6 copy.195
  286.2 16.5 %collective-permute-start.2 = (bf16[1,8,12,2048]{3,1,2,0:T(8,128)(2,1)S(1)}, bf16[1,8,12,2048]{3,1,2,0:T(8,128)(2,1)S(1)}, u32[]{:S(2)}, u32[]{:S(2)}) collective-permute-start(bf16[1,8,12,2048]{3,1,2,0:T(8,128)(2,1)S(1)} %bitcast.181), channel_id=1, source_target_pairs={{0,3},{1,4},{2,5},{3,6},{4,7},{5,8},{6,9},{7,10},{8,11},{9,12},{10... | collective-permute-start | bytes 1179656 | tf_op jit(solution)/shard_map/ppermute | solution.py:36
  302.8 1.6 copy.194
  305.3 2.3 collective-permute-start.4
  311.9 1.2 bitcast_dynamic-update-slice_fusion.15
  313.1 2.7 collective-permute-start.5
  315.8 0.8 bitcast_dynamic-update-slice_fusion.14
  316.6 3.0 collective-permute-start.6
  320.4 1.8 collective-permute-start.7
  322.2 0.8 bitcast_dynamic-update-slice_fusion.12
  323.0 7.0 %collective-permute-start.8 = (bf16[1,8,12,2048]{3,1,2,0:T(8,128)(2,1)S(1)}, bf16[1,8,12,2048]{3,1,2,0:T(8,128)(2,1)S(1)}, u32[]{:S(2)}, u32[]{:S(2)}) collective-permute-start(bf16[1,8,12,2048]{3,1,2,0:T(8,128)(2,1)S(1)} %bitcast.175), channel_id=1, source_target_pairs={{0,9},{1,10},{2,11},{3,12},{4,13},{5,14},{6,15},{7,0},{8,1},{9,2},... | collective-permute-start | bytes 1179656 | tf_op jit(solution)/shard_map/ppermute | solution.py:36
  330.7 39.1 %collective-permute-done.4 = bf16[1,8,12,2048]{3,1,2,0:T(8,128)(2,1)S(1)} collective-permute-done((bf16[1,8,12,2048]{3,1,2,0:T(8,128)(2,1)S(1)}, bf16[1,8,12,2048]{3,1,2,0:T(8,128)(2,1)S(1)}, u32[]{:S(2)}, u32[]{:S(2)}) %collective-permute-start.4) | collective-permute-done | bytes 393248 | tf_op jit(solution)/shard_map/ppermute | solution.py:36
  369.9 2.1 collective-permute-start.9
  372.0 0.8 bitcast_dynamic-update-slice_fusion.10
  372.8 1.7 collective-permute-done.5
  374.5 15.7 %collective-permute-start.10 = (bf16[1,8,12,2048]{3,1,2,0:T(8,128)(2,1)S(1)}, bf16[1,8,12,2048]{3,1,2,0:T(8,128)(2,1)S(1)}, u32[]{:S(2)}, u32[]{:S(2)}) collective-permute-start(bf16[1,8,12,2048]{3,1,2,0:T(8,128)(2,1)S(1)} %bitcast.173), channel_id=1, source_target_pairs={{0,11},{1,12},{2,13},{3,14},{4,15},{5,0},{6,1},{7,2},{8,3},{9,4},{... | collective-permute-start | bytes 1179656 | tf_op jit(solution)/shard_map/ppermute | solution.py:36
  391.0 32.6 %collective-permute-start.11 = (bf16[1,8,12,2048]{3,1,2,0:T(8,128)(2,1)S(1)}, bf16[1,8,12,2048]{3,1,2,0:T(8,128)(2,1)S(1)}, u32[]{:S(2)}, u32[]{:S(2)}) collective-permute-start(bf16[1,8,12,2048]{3,1,2,0:T(8,128)(2,1)S(1)} %bitcast.172), channel_id=1, source_target_pairs={{0,12},{1,13},{2,14},{3,15},{4,0},{5,1},{6,2},{7,3},{8,4},{9,5},{1... | collective-permute-start | bytes 1179656 | tf_op jit(solution)/shard_map/ppermute | solution.py:36
  423.6 0.8 bitcast_dynamic-update-slice_fusion.8
  425.6 7.8 %collective-permute-start.13 = (bf16[1,8,12,2048]{3,1,2,0:T(8,128)(2,1)S(1)}, bf16[1,8,12,2048]{3,1,2,0:T(8,128)(2,1)S(1)}, u32[]{:S(2)}, u32[]{:S(2)}) collective-permute-start(bf16[1,8,12,2048]{3,1,2,0:T(8,128)(2,1)S(1)} %bitcast.170), channel_id=1, source_target_pairs={{0,14},{1,15},{2,0},{3,1},{4,2},{5,3},{6,4},{7,5},{8,6},{9,7},{10,... | collective-permute-start | bytes 1179656 | tf_op jit(solution)/shard_map/ppermute | solution.py:36
  434.1 6.2 %collective-permute-start.14 = (bf16[1,8,12,2048]{3,1,2,0:T(8,128)(2,1)S(1)}, bf16[1,8,12,2048]{3,1,2,0:T(8,128)(2,1)S(1)}, u32[]{:S(2)}, u32[]{:S(2)}) collective-permute-start(bf16[1,8,12,2048]{3,1,2,0:T(8,128)(2,1)S(1)} %bitcast.169), channel_id=1, source_target_pairs={{0,15},{1,0},{2,1},{3,2},{4,3},{5,4},{6,5},{7,6},{8,7},{9,8},{10,9... | collective-permute-start | bytes 1179656 | tf_op jit(solution)/shard_map/ppermute | solution.py:36
  441.1 0.8 bitcast_dynamic-update-slice_fusion.4
  441.8 0.8 bitcast_dynamic-update-slice_fusion.3
  442.6 0.8 bitcast_dynamic-update-slice_fusion.2
  443.4 7.3 %collective-permute-done.13 = bf16[1,8,12,2048]{3,1,2,0:T(8,128)(2,1)S(1)} collective-permute-done((bf16[1,8,12,2048]{3,1,2,0:T(8,128)(2,1)S(1)}, bf16[1,8,12,2048]{3,1,2,0:T(8,128)(2,1)S(1)}, u32[]{:S(2)}, u32[]{:S(2)}) %collective-permute-start.13) | collective-permute-done | bytes 393248 | tf_op jit(solution)/shard_map/ppermute | solution.py:36
  450.7 0.8 bitcast_dynamic-update-slice_fusion.1
  451.5 4.8 collective-permute-done.14
  456.3 0.8 bitcast_dynamic-update-slice_fusion
  457.1 6.4 %gather_fusion.1 = bf16[16,8,12,2048]{3,1,2,0:T(8,128)(2,1)} fusion(bf16[16,8,12,2048]{3,1,2,0:T(8,128)(2,1)} %bitcast.52, s32[1024]{0:T(1024)S(1)} %pad_clamp_fusion.1), kind=kCustom, calls=%fused_computation.1 | custom fusion | bytes 12582976 | tf_op jit(solution)/shard_map/gather | solution.py:37
  463.5 13.7 %copy.137 = f32[16,8,12,2048]{3,2,1,0:T(8,128)} copy(bf16[16,8,12,2048]{3,1,2,0:T(8,128)(2,1)} %gather_fusion.1) | data formatting | bytes 18874368 | tf_op jit(solution)/shard_map/convert_element_type | solution.py:194
  477.2 15.5 %reshape.459 = f32[1536,2048]{1,0:T(8,128)} reshape(f32[16,8,12,2048]{3,2,1,0:T(8,128)} %copy.137) | data formatting | bytes 25165824 | tf_op jit(solution)/shard_map/convert_element_type | solution.py:194
  492.7 23.1 %scatter_custom_fusion.2 = f32[129,2048]{1,0:T(8,128)} fusion(s32[1536]{0:T(1024)S(1)} %get-tuple-element.30, f32[1536,2048]{1,0:T(8,128)} %reshape.459, f32[1536]{0:T(1024)S(1)} %bitcast.186, f32[]{:T(128)} %constant.206.clone.1), kind=kCustom, calls=%fused_computation.7 | custom fusion | flops 6291456 | bytes 13647876 | tf_op jit(solution)/shard_map/scatter-add | solution.py:195
  515.9 2.9 fusion.20
  518.8 1.1 convert_element_type.110
  519.9 12.4 %reduce-scatter.2.cloned.1.call-done = bf16[128,1024]{1,0:T(8,128)(2,1)} async-done(((bf16[128,2048]{1,0:T(8,128)(2,1)}), bf16[128,1024]{1,0:T(8,128)(2,1)}) %reduce-scatter.2.cloned.1.call-update) | async-done | bytes 262160 | tf_op jit(solution)/shard_map/reduce_scatter | solution.py:204
  532.3 1.9 add_convert_fusion
  (91 shorter events, 15.0 us)
Async XLA Ops:
  6.5 509.3 %copy-start = (bf16[704,2048]{1,0:T(8,128)(2,1)S(1)}, bf16[704,2048]{1,0:T(8,128)(2,1)}, u32[]{:S(2)}) copy-start(bf16[704,2048]{1,0:T(8,128)(2,1)} %param.29) | copy-start | bytes 8650756
  6.5 15.1 %copy-start.10 = (s32[4]{0:T(128)S(1)}, s32[4]{0:T(128)}, u32[]{:S(2)}) copy-start(s32[4]{0:T(128)} %param.18) | copy-start | bytes 52
  24.8 2.0 copy-start.6
  26.9 2.2 copy-start.5
  26.9 4.0 copy-start.7
  29.1 11.8 %copy-start.9 = (f32[2048]{0:T(1024)S(1)}, f32[2048]{0:T(1024)}, u32[]{:S(2)}) copy-start(f32[2048]{0:T(1024)} %param.21) | copy-start | bytes 24580
  40.1 0.8 copy-start.1
  41.1 0.8 copy-start.3
  70.3 8.5 %copy-start.4 = (bf16[128,2048]{1,0:T(8,128)(2,1)S(1)}, bf16[128,2048]{1,0:T(8,128)(2,1)}, u32[]{:S(2)}) copy-start(bf16[128,2048]{1,0:T(8,128)(2,1)} %copy-done.3) | copy-start | bytes 1572868
  70.3 9.7 %copy-start.8 = (s32[128,6]{0,1:T(8,128)S(1)}, s32[128,6]{0,1:T(8,128)}, u32[]{:S(2)}) copy-start(s32[128,6]{0,1:T(8,128)} %param.23) | copy-start | bytes 9220
  70.3 128.4 %all-to-all-start = ((bf16[16,8,12,2048]{3,1,2,0:T(8,128)(2,1)}), bf16[16,8,12,2048]{3,1,2,0:T(8,128)(2,1)}, u32[]{:S(2)}, u32[]{:S(2)}) async-start(bf16[16,8,12,2048]{3,1,2,0:T(8,128)(2,1)} %copy.118), calls=%async_computation | async-start | bytes 12582912 | tf_op jit(solution)/shard_map/all_to_all | solution.py:179
  78.6 453.7 %reduce-scatter.2.cloned.1.call-start = ((), (), s32[]{:S(2)}) async-start(), calls=%async_computation.2 | async-start | bytes 786432 | tf_op jit(solution)/shard_map/reduce_scatter | solution.py:204
  271.8 41.3 %collective-permute-start = (bf16[1,8,12,2048]{3,1,2,0:T(8,128)(2,1)S(1)}, bf16[1,8,12,2048]{3,1,2,0:T(8,128)(2,1)S(1)}, u32[]{:S(2)}, u32[]{:S(2)}) collective-permute-start(bf16[1,8,12,2048]{3,1,2,0:T(8,128)(2,1)S(1)} %bitcast.183), channel_id=1, source_target_pairs={{0,1},{1,2},{2,3},{3,4},{4,5},{5,6},{6,7},{7,8},{8,9},{9,10},{10,1... | collective-permute-start | bytes 1179656 | tf_op jit(solution)/shard_map/ppermute | solution.py:36
  275.7 40.8 %collective-permute-start.1 = (bf16[1,8,12,2048]{3,1,2,0:T(8,128)(2,1)S(1)}, bf16[1,8,12,2048]{3,1,2,0:T(8,128)(2,1)S(1)}, u32[]{:S(2)}, u32[]{:S(2)}) collective-permute-start(bf16[1,8,12,2048]{3,1,2,0:T(8,128)(2,1)S(1)} %bitcast.182), channel_id=1, source_target_pairs={{0,2},{1,3},{2,4},{3,5},{4,6},{5,7},{6,8},{7,9},{8,10},{9,11},{10,... | collective-permute-start | bytes 1179656 | tf_op jit(solution)/shard_map/ppermute | solution.py:36
  286.2 34.1 %collective-permute-start.2 = (bf16[1,8,12,2048]{3,1,2,0:T(8,128)(2,1)S(1)}, bf16[1,8,12,2048]{3,1,2,0:T(8,128)(2,1)S(1)}, u32[]{:S(2)}, u32[]{:S(2)}) collective-permute-start(bf16[1,8,12,2048]{3,1,2,0:T(8,128)(2,1)S(1)} %bitcast.181), channel_id=1, source_target_pairs={{0,3},{1,4},{2,5},{3,6},{4,7},{5,8},{6,9},{7,10},{8,11},{9,12},{10... | collective-permute-start | bytes 1179656 | tf_op jit(solution)/shard_map/ppermute | solution.py:36
  304.3 18.7 %collective-permute-start.3 = (bf16[1,8,12,2048]{3,1,2,0:T(8,128)(2,1)S(1)}, bf16[1,8,12,2048]{3,1,2,0:T(8,128)(2,1)S(1)}, u32[]{:S(2)}, u32[]{:S(2)}) collective-permute-start(bf16[1,8,12,2048]{3,1,2,0:T(8,128)(2,1)S(1)} %bitcast.180), channel_id=1, source_target_pairs={{0,4},{1,5},{2,6},{3,7},{4,8},{5,9},{6,10},{7,11},{8,12},{9,13},{1... | collective-permute-start | bytes 1179656 | tf_op jit(solution)/shard_map/ppermute | solution.py:36
  305.3 64.6 %collective-permute-start.4 = (bf16[1,8,12,2048]{3,1,2,0:T(8,128)(2,1)S(1)}, bf16[1,8,12,2048]{3,1,2,0:T(8,128)(2,1)S(1)}, u32[]{:S(2)}, u32[]{:S(2)}) collective-permute-start(bf16[1,8,12,2048]{3,1,2,0:T(8,128)(2,1)S(1)} %bitcast.179), channel_id=1, source_target_pairs={{0,5},{1,6},{2,7},{3,8},{4,9},{5,10},{6,11},{7,12},{8,13},{9,14},{... | collective-permute-start | bytes 1179656 | tf_op jit(solution)/shard_map/ppermute | solution.py:36
  313.1 61.4 %collective-permute-start.5 = (bf16[1,8,12,2048]{3,1,2,0:T(8,128)(2,1)S(1)}, bf16[1,8,12,2048]{3,1,2,0:T(8,128)(2,1)S(1)}, u32[]{:S(2)}, u32[]{:S(2)}) collective-permute-start(bf16[1,8,12,2048]{3,1,2,0:T(8,128)(2,1)S(1)} %bitcast.178), channel_id=1, source_target_pairs={{0,6},{1,7},{2,8},{3,9},{4,10},{5,11},{6,12},{7,13},{8,14},{9,15},... | collective-permute-start | bytes 1179656 | tf_op jit(solution)/shard_map/ppermute | solution.py:36
  316.6 74.4 %collective-permute-start.6 = (bf16[1,8,12,2048]{3,1,2,0:T(8,128)(2,1)S(1)}, bf16[1,8,12,2048]{3,1,2,0:T(8,128)(2,1)S(1)}, u32[]{:S(2)}, u32[]{:S(2)}) collective-permute-start(bf16[1,8,12,2048]{3,1,2,0:T(8,128)(2,1)S(1)} %bitcast.177), channel_id=1, source_target_pairs={{0,7},{1,8},{2,9},{3,10},{4,11},{5,12},{6,13},{7,14},{8,15},{9,0},... | collective-permute-start | bytes 1179656 | tf_op jit(solution)/shard_map/ppermute | solution.py:36
  320.4 104.0 %collective-permute-start.7 = (bf16[1,8,12,2048]{3,1,2,0:T(8,128)(2,1)S(1)}, bf16[1,8,12,2048]{3,1,2,0:T(8,128)(2,1)S(1)}, u32[]{:S(2)}, u32[]{:S(2)}) collective-permute-start(bf16[1,8,12,2048]{3,1,2,0:T(8,128)(2,1)S(1)} %bitcast.176), channel_id=1, source_target_pairs={{0,8},{1,9},{2,10},{3,11},{4,12},{5,13},{6,14},{7,15},{8,0},{9,1},... | collective-permute-start | bytes 1179656 | tf_op jit(solution)/shard_map/ppermute | solution.py:36
  323.0 102.6 %collective-permute-start.8 = (bf16[1,8,12,2048]{3,1,2,0:T(8,128)(2,1)S(1)}, bf16[1,8,12,2048]{3,1,2,0:T(8,128)(2,1)S(1)}, u32[]{:S(2)}, u32[]{:S(2)}) collective-permute-start(bf16[1,8,12,2048]{3,1,2,0:T(8,128)(2,1)S(1)} %bitcast.175), channel_id=1, source_target_pairs={{0,9},{1,10},{2,11},{3,12},{4,13},{5,14},{6,15},{7,0},{8,1},{9,2},... | collective-permute-start | bytes 1179656 | tf_op jit(solution)/shard_map/ppermute | solution.py:36
  369.9 64.2 %collective-permute-start.9 = (bf16[1,8,12,2048]{3,1,2,0:T(8,128)(2,1)S(1)}, bf16[1,8,12,2048]{3,1,2,0:T(8,128)(2,1)S(1)}, u32[]{:S(2)}, u32[]{:S(2)}) collective-permute-start(bf16[1,8,12,2048]{3,1,2,0:T(8,128)(2,1)S(1)} %bitcast.174), channel_id=1, source_target_pairs={{0,10},{1,11},{2,12},{3,13},{4,14},{5,15},{6,0},{7,1},{8,2},{9,3},... | collective-permute-start | bytes 1179656 | tf_op jit(solution)/shard_map/ppermute | solution.py:36
  374.5 66.6 %collective-permute-start.10 = (bf16[1,8,12,2048]{3,1,2,0:T(8,128)(2,1)S(1)}, bf16[1,8,12,2048]{3,1,2,0:T(8,128)(2,1)S(1)}, u32[]{:S(2)}, u32[]{:S(2)}) collective-permute-start(bf16[1,8,12,2048]{3,1,2,0:T(8,128)(2,1)S(1)} %bitcast.173), channel_id=1, source_target_pairs={{0,11},{1,12},{2,13},{3,14},{4,15},{5,0},{6,1},{7,2},{8,3},{9,4},{... | collective-permute-start | bytes 1179656 | tf_op jit(solution)/shard_map/ppermute | solution.py:36
  391.0 50.8 %collective-permute-start.11 = (bf16[1,8,12,2048]{3,1,2,0:T(8,128)(2,1)S(1)}, bf16[1,8,12,2048]{3,1,2,0:T(8,128)(2,1)S(1)}, u32[]{:S(2)}, u32[]{:S(2)}) collective-permute-start(bf16[1,8,12,2048]{3,1,2,0:T(8,128)(2,1)S(1)} %bitcast.172), channel_id=1, source_target_pairs={{0,12},{1,13},{2,14},{3,15},{4,0},{5,1},{6,2},{7,3},{8,4},{9,5},{1... | collective-permute-start | bytes 1179656 | tf_op jit(solution)/shard_map/ppermute | solution.py:36
  424.3 18.3 %collective-permute-start.12 = (bf16[1,8,12,2048]{3,1,2,0:T(8,128)(2,1)S(1)}, bf16[1,8,12,2048]{3,1,2,0:T(8,128)(2,1)S(1)}, u32[]{:S(2)}, u32[]{:S(2)}) collective-permute-start(bf16[1,8,12,2048]{3,1,2,0:T(8,128)(2,1)S(1)} %bitcast.171), channel_id=1, source_target_pairs={{0,13},{1,14},{2,15},{3,0},{4,1},{5,2},{6,3},{7,4},{8,5},{9,6},{10... | collective-permute-start | bytes 1179656 | tf_op jit(solution)/shard_map/ppermute | solution.py:36
  425.6 25.1 %collective-permute-start.13 = (bf16[1,8,12,2048]{3,1,2,0:T(8,128)(2,1)S(1)}, bf16[1,8,12,2048]{3,1,2,0:T(8,128)(2,1)S(1)}, u32[]{:S(2)}, u32[]{:S(2)}) collective-permute-start(bf16[1,8,12,2048]{3,1,2,0:T(8,128)(2,1)S(1)} %bitcast.170), channel_id=1, source_target_pairs={{0,14},{1,15},{2,0},{3,1},{4,2},{5,3},{6,4},{7,5},{8,6},{9,7},{10,... | collective-permute-start | bytes 1179656 | tf_op jit(solution)/shard_map/ppermute | solution.py:36
  434.1 22.2 %collective-permute-start.14 = (bf16[1,8,12,2048]{3,1,2,0:T(8,128)(2,1)S(1)}, bf16[1,8,12,2048]{3,1,2,0:T(8,128)(2,1)S(1)}, u32[]{:S(2)}, u32[]{:S(2)}) collective-permute-start(bf16[1,8,12,2048]{3,1,2,0:T(8,128)(2,1)S(1)} %bitcast.169), channel_id=1, source_target_pairs={{0,15},{1,0},{2,1},{3,2},{4,3},{5,4},{6,5},{7,6},{8,7},{9,8},{10,9... | collective-permute-start | bytes 1179656 | tf_op jit(solution)/shard_map/ppermute | solution.py:36
  492.7 26.1 %copy-start.2 = (bf16[128,2048]{1,0:T(8,128)(2,1)S(1)}, bf16[128,2048]{1,0:T(8,128)(2,1)}, u32[]{:S(2)}) copy-start(bf16[128,2048]{1,0:T(8,128)(2,1)} %copy-done.1) | copy-start | bytes 1572868
Sparse Core Ops, SparseCore 0:
  518.9 13.3 reduce-scatter.1
